TPU v7x, 128 devices: a whole 4x4x4 slice. The times are simulated.
128 devices in a mesh: seq: 16 (over x_hi, z, core), blk: 8 (over y, x_lo).
Axes of the slice: x: 4 (x_hi: 2, x_lo: 2; x = x_hi * 2 + x_lo), y: 4, z: 4, core: 2. Of those that a mesh axis runs over, the one named last changes fastest.
Arguments:
- tokens: bfloat16 [16384, 3072], P(('seq', 'blk')), may hold values from -8.6 to 8.6
- project_weight: bfloat16 [3, 3072, 2048], P(None, None, 'seq')
- noisy_latent: float32 [16384, 64], P(('seq', 'blk')), may hold values from -6 to 6
- final_weight: bfloat16 [2048, 64], replicated, may hold values from -0.5 to 0.5
- conv_weight: bfloat16 [432, 512], replicated, may hold values from -0.3125 to 0.3125
- norm_gain: float32 [512], replicated, may hold values from 0.1 to 1.9
- norm_shift: float32 [512], replicated, may hold values from -3 to 3
- owner_count: int32 [128], replicated, may hold values from 1 to 4, 256 in all
- intersection: int32 [256, 4], replicated, may hold values from 0 to 127, as said below
Outputs:
- decoded: bfloat16 [128, 4, 512, 2048], P(('seq', 'blk'))
Inputs may be any that keep to these rules, and one draw needn't show every extreme that they name: Owner o holds pixel tiles s to s + owner_count[o] - 1, s the sum of the counts below o; the counts sum to 256 and one owner holds exactly 4. `intersection`: row p names the four latent tiles of a 2 x 2 block of neighbouring tiles on a grid of 16 rows by 8 columns, tile r * 8 + c at row r, column c, in the order top left, top right, bottom left, bottom right.
All inputs are finite; a program needn't handle non-finite values.
Results may differ from a plain program's by a relative error of at most 0.014.
Values may be sent and summed in bfloat16 or wider, within the bound.
No kernel may reach another device: no remote copies, remote signals or barrier semaphores. Data moves between devices by JAX's collectives and lax.ppermute only.
A program may use at most 128 MiB of HBM per device.

v0:
```python
import jax
import jax.numpy as jnp
from jax import lax
from jax.sharding import PartitionSpec as P

HEAD_DIM = 128
LATENT_CH = 16
GROUPS = 32
TILE_F = 2
TILE_PH = 8
TILE_PW = 8
MAXPIX = 4


scale_factor = 0.476986
step_size = 0.25
norm_eps = 1e-06


def decode_tile(all_tiles, tile_ids, conv_weight, norm_gain, norm_shift):
    pieces = all_tiles[tile_ids]
    upper = jnp.concatenate([pieces[0], pieces[1]], axis=3)
    lower = jnp.concatenate([pieces[2], pieces[3]], axis=3)
    region = jnp.concatenate([upper, lower], axis=2)
    padded = jnp.pad(region, ((0, 0), (2, 0), (1, 1), (1, 1)), mode="edge")
    frames = region.shape[1]
    height = region.shape[2]
    breadth = region.shape[3]
    tap_list = []
    for tap_time in range(3):
        for tap_row in range(3):
            for tap_col in range(3):
                window = padded[
                    :,
                    tap_time : tap_time + frames,
                    tap_row : tap_row + height,
                    tap_col : tap_col + breadth,
                ]
                tap_list.append(window.reshape(region.shape[0], -1))
    patches = jnp.concatenate(tap_list, axis=0)
    convolved = lax.dot_general(
        conv_weight, patches, (((0,), (0,)), ((), ())), preferred_element_type=jnp.float32
    )
    channels = convolved.shape[0]
    grouped = convolved.reshape(GROUPS, channels // GROUPS, -1)
    group_mean = jnp.mean(grouped, axis=(1, 2), keepdims=True)
    group_var = jnp.mean(jnp.square(grouped - group_mean), axis=(1, 2), keepdims=True)
    normed = ((grouped - group_mean) * lax.rsqrt(group_var + norm_eps)).reshape(channels, -1)
    normed = normed * norm_gain[:, None] + norm_shift[:, None]
    return jax.nn.silu(normed).astype(jnp.bfloat16)


def body(
    tokens,
    project_weight,
    noisy_latent,
    final_weight,
    conv_weight,
    norm_gain,
    norm_shift,
    owner_count,
    intersection,
):
    head_local = project_weight.shape[2] // HEAD_DIM
    joined_weight = project_weight.transpose(1, 0, 2).reshape(
        project_weight.shape[1], 3 * project_weight.shape[2]
    )
    projected = jnp.dot(
        lax.all_gather(tokens, "seq", axis=0, tiled=True),
        joined_weight,
        preferred_element_type=jnp.float32,
    ).astype(jnp.bfloat16)
    projected = projected.reshape(-1, 3, head_local, HEAD_DIM)
    queries = projected[:, 0]
    key_rows = projected[:, 1]
    value_rows = projected[:, 2]
    group_len = queries.shape[0]
    inv_root = HEAD_DIM ** (-0.5)
    initial = (
        jnp.full((head_local, group_len), -1e30, jnp.float32),
        jnp.zeros((head_local, group_len), jnp.float32),
        jnp.zeros((head_local, group_len, HEAD_DIM), jnp.float32),
    )
    running = initial
    key_piece = lax.all_gather(key_rows, "blk", axis=0, tiled=True)
    value_piece = lax.all_gather(value_rows, "blk", axis=0, tiled=True)
    piece_len = key_piece.shape[0]
    block_len = min(piece_len, group_len)
    block_count = piece_len // block_len
    key_blocks = key_piece.reshape(block_count, block_len, head_local, HEAD_DIM)
    value_blocks = value_piece.reshape(block_count, block_len, head_local, HEAD_DIM)

    def one_block(softmax_state, block_pair):
        run_max, run_sum, run_acc = softmax_state
        key_block, value_block = block_pair
        scores = (
            jnp.einsum("qhd,khd->hqk", queries, key_block, preferred_element_type=jnp.float32)
            * inv_root
        )
        new_max = jnp.maximum(run_max, jnp.max(scores, axis=2))
        rescale = jnp.exp(run_max - new_max)
        exp_scores = jnp.exp(scores - new_max[:, :, None])
        run_sum = run_sum * rescale + jnp.sum(exp_scores, axis=2)
        run_acc = run_acc * rescale[:, :, None] + jnp.einsum(
            "hqk,khd->hqd",
            exp_scores.astype(jnp.bfloat16),
            value_block,
            preferred_element_type=jnp.float32,
        )
        return ((new_max, run_sum, run_acc), None)

    running, unused = lax.scan(one_block, running, (key_blocks, value_blocks))
    attended = (running[2] / running[1][:, :, None]).astype(jnp.bfloat16)
    by_token = attended.transpose(1, 0, 2)
    regrouped = lax.all_to_all(by_token, "seq", split_axis=0, concat_axis=1, tiled=True)
    velocity = jnp.dot(
        regrouped.reshape(regrouped.shape[0], -1), final_weight, preferred_element_type=jnp.float32
    )
    latent = (noisy_latent - step_size * velocity) / scale_factor
    own_tile = latent.reshape(TILE_F, TILE_PH, TILE_PW, LATENT_CH, 2, 2).transpose(3, 0, 1, 4, 2, 5)
    own_tile = own_tile.reshape(1, LATENT_CH, -1).astype(jnp.bfloat16)
    owner_rank = lax.axis_index("seq") * lax.axis_size("blk") + lax.axis_index("blk")
    count_ends = jnp.cumsum(owner_count, dtype=jnp.int32)
    all_tiles = lax.all_gather(own_tile, ("seq", "blk"), axis=0, tiled=True)
    all_tiles = all_tiles.reshape(-1, LATENT_CH, TILE_F, 2 * TILE_PH, 2 * TILE_PW)
    own_count = owner_count[owner_rank]
    first_tile = count_ends[owner_rank] - own_count
    last_pixel = intersection.shape[0] - 1
    region_vox = 16 * tokens.shape[0]

    def decode_slot(pixel_index):
        return decode_tile(all_tiles, intersection[pixel_index], conv_weight, norm_gain, norm_shift)

    def empty_slot(pixel_index):
        return jnp.zeros((conv_weight.shape[1], region_vox), jnp.bfloat16)

    slot_outputs = []
    for slot_index in range(MAXPIX):
        pixel_index = jnp.minimum(first_tile + slot_index, last_pixel)
        slot_outputs.append(lax.cond(slot_index < own_count, decode_slot, empty_slot, pixel_index))
    return jnp.stack(slot_outputs)[None]


def solution(mesh):
    return jax.shard_map(
        body,
        mesh=mesh,
        in_specs=(
            P(("seq", "blk"), None),
            P(None, None, "seq"),
            P(("seq", "blk"), None),
            P(),
            P(),
            P(),
            P(),
            P(),
            P(),
        ),
        out_specs=P(("seq", "blk"), None, None, None),
        check_vma=False,
    )
```

profile of v0, /device:TPU:19, one launch (start us, length us, event | category | flops | bytes accessed | tf_op | source)
XLA Modules:
  0.0 1230.9 jit_solution(9489557946939757063)
XLA Ops:
  11.6 90.9 %all-gather.7.cloned.1.call-done = bf16[2048,3072]{1,0:T(8,128)(2,1)} async-done(((bf16[128,3072]{1,0:T(8,128)(2,1)}), bf16[2048,3072]{1,0:T(8,128)(2,1)}) %all-gather.7.cloned.1.call-update) | async-done | bytes 12582928 | tf_op jit(solution)/shard_map/all_gather | solution.py:69
  102.5 8.8 convolution_convert_fusion
  113.9 86.2 %all-gather.11.cloned.1.call-done = bf16[16384,1,1,128]{3,0,2,1:T(8,128)(2,1)} async-done(((bf16[2048,1,1,128]{3,0,2,1:T(8,128)(2,1)}), bf16[16384,1,1,128]{3,0,2,1:T(8,128)(2,1)}) %all-gather.11.cloned.1.call-update) | async-done | bytes 4194320 | tf_op jit(solution)/shard_map/all_gather | solution.py:85
  200.1 92.4 %all-gather.13.cloned.1.call-done = bf16[16384,1,1,128]{3,0,2,1:T(8,128)(2,1)} async-done(((bf16[2048,1,1,128]{3,0,2,1:T(8,128)(2,1)}), bf16[16384,1,1,128]{3,0,2,1:T(8,128)(2,1)}) %all-gather.13.cloned.1.call-update) | async-done | bytes 4194320 | tf_op jit(solution)/shard_map/all_gather | solution.py:86
  292.5 202.2 %while.15 = (s32[]{:T(128)}, f32[1,2048]{1,0:T(1,128)S(1)}, f32[1,2048]{1,0:T(1,128)S(1)}, f32[1,2048,128]{2,1,0:T(8,128)S(1)}, bf16[8,2048,1,128]{3,1,2,0:T(8,1...) while((s32[]{:T(128)}, f32[1,2048]{1,0:T(1,128)S(1)}, ...), condition=%wide.region_4.5_spmd.clone, body=%wide.region_1.4_spmd.clone.sunk | while | flops 2181834752 | bytes 54133860 | solution.py:112
  292.5 9.1 multiply_reduce_fusion.6
  301.6 8.5 fusion.100
  317.8 9.1 multiply_reduce_fusion.6
  326.9 8.5 fusion.100
  343.0 9.1 multiply_reduce_fusion.6
  352.1 8.5 fusion.100
  360.7 7.5 fusion.102
  368.3 9.1 multiply_reduce_fusion.6
  377.4 8.5 fusion.100
  393.6 9.1 multiply_reduce_fusion.6
  402.7 8.5 fusion.100
  418.9 9.1 multiply_reduce_fusion.6
  428.0 8.5 fusion.100
  444.1 9.1 multiply_reduce_fusion.6
  453.2 8.5 fusion.100
  469.4 9.1 multiply_reduce_fusion.6
  478.5 8.5 fusion.100
  496.7 31.1 %all_to_all.15 = bf16[16,2,8192]{2,1,0:T(2,128)(2,1)S(1)} all-to-all(bf16[16,2,8192]{2,1,0:T(2,128)(2,1)S(1)} %reshape.654), channel_id=1, replica_groups=mesh['seq'=16,'blk'=8] {'seq'}, dimensions={0} | all-to-all | bytes 1048576 | tf_op jit(solution)/shard_map/all_to_all | solution.py:115
  535.3 294.8 %all-gather.9.cloned.1.call-done = bf16[128,16,512]{2,1,0:T(8,128)(2,1)} async-done(((bf16[1,16,512]{2,1,0:T(8,128)(2,1)}), bf16[128,16,512]{2,1,0:T(8,128)(2,1)}) %all-gather.9.cloned.1.call-update) | async-done | bytes 2097168 | tf_op jit(solution)/shard_map/all_gather | solution.py:124
  833.6 99.1 %conditional.4 = (bf16[1,512,2048]{2,1,0:T(8,128)(2,1)}) conditional(s32[]{:T(128)} %convert_element_type.55, () %tuple.41, (s32[]{:T(128)}, s32[256,4]{0,1:T(4,128)S(1)}, bf16[128,16,2,16,16]{0,4,3,2,1:T(8,128)(2,1)S(1)}, bf16[432,512]{1,0:T(8,128)(2,1)}, f32[512]{0:T(512)S(1)}, /*index=5*/f32[512]{0:T(512)S(1)}) %tuple.293), branch_computations={%region_5.6_spmd, %region_6.11_spmd} | conditional | flops 925127744 | bytes 38638832 | solution.py:140
  833.8 22.6 %copy.106 = bf16[128,16,2,16,16]{4,3,2,1,0:T(8,128)(2,1)} copy(bf16[128,16,2,16,16]{0,4,3,2,1:T(8,128)(2,1)S(1)} %get-tuple-element.297) | data formatting | bytes 4194304 | tf_op jit(solution)/shard_map
  932.7 99.1 %conditional.5 = (bf16[1,512,2048]{2,1,0:T(8,128)(2,1)}) conditional(s32[]{:T(128)} %convert_element_type.62, () %tuple.44, (s32[]{:T(128)}, s32[256,4]{0,1:T(4,128)S(1)}, bf16[128,16,2,16,16]{0,4,3,2,1:T(8,128)(2,1)S(1)}, bf16[432,512]{1,0:T(8,128)(2,1)}, f32[512]{0:T(512)S(1)}, /*index=5*/f32[512]{0:T(512)S(1)}) %tuple.294), branch_computations={%region_11.12_spmd, %region_12.0_spmd} | conditional | flops 925127744 | bytes 38638848 | solution.py:140
  933.0 22.6 %copy.108 = bf16[128,16,2,16,16]{4,3,2,1,0:T(8,128)(2,1)} copy(bf16[128,16,2,16,16]{0,4,3,2,1:T(8,128)(2,1)S(1)} %get-tuple-element.303) | data formatting | bytes 4194304 | tf_op jit(solution)/shard_map
  1031.8 99.4 %conditional.6 = (bf16[1,512,2048]{2,1,0:T(8,128)(2,1)}) conditional(s32[]{:T(128)} %convert_element_type.63, () %tuple.45, (s32[]{:T(128)}, s32[256,4]{0,1:T(4,128)S(1)}, bf16[128,16,2,16,16]{0,4,3,2,1:T(8,128)(2,1)S(1)}, bf16[432,512]{1,0:T(8,128)(2,1)}, f32[512]{0:T(512)S(1)}, /*index=5*/f32[512]{0:T(512)S(1)}) %tuple.295), branch_computations={%region_17.18_spmd, %region_18.23_spmd} | conditional | flops 925127744 | bytes 38638848 | solution.py:140
  1032.0 22.6 %copy.110 = bf16[128,16,2,16,16]{4,3,2,1,0:T(8,128)(2,1)} copy(bf16[128,16,2,16,16]{0,4,3,2,1:T(8,128)(2,1)S(1)} %get-tuple-element.309) | data formatting | bytes 4194304 | tf_op jit(solution)/shard_map
  1131.3 85.6 %conditional.7 = (bf16[1,512,2048]{2,1,0:T(8,128)(2,1)}) conditional(s32[]{:T(128)} %convert_element_type.64, () %tuple.46, (s32[]{:T(128)}, s32[256,4]{0,1:T(4,128)S(1)}, bf16[128,16,2,16,16]{0,4,3,2,1:T(8,128)(2,1)S(1)}, bf16[432,512]{1,0:T(8,128)(2,1)}, f32[512]{0:T(512)S(1)}, /*index=5*/f32[512]{0:T(512)S(1)}) %tuple.296), branch_computations={%region_23.24_spmd, %region_24.29_spmd} | conditional | flops 925127744 | bytes 42243552 | solution.py:140
  1131.5 22.6 %copy.112 = bf16[128,16,2,16,16]{4,3,2,1,0:T(8,128)(2,1)} copy(bf16[128,16,2,16,16]{0,4,3,2,1:T(8,128)(2,1)S(1)} %get-tuple-element.315) | data formatting | bytes 4194304 | tf_op jit(solution)/shard_map
  (462 shorter events, 368.0 us)
Async XLA Ops:
  6.5 522.2 %copy-start = (bf16[2048,64]{0,1:T(8,128)(2,1)S(1)}, bf16[2048,64]{0,1:T(8,128)(2,1)}, u32[]{:S(2)}) copy-start(bf16[2048,64]{0,1:T(8,128)(2,1)} %param.22) | copy-start | bytes 786436
  6.5 95.9 %all-gather.7.cloned.1.call-start = ((), (), s32[]{:S(2)}) async-start(), calls=%async_computation.1 | async-start | bytes 13369344 | tf_op jit(solution)/shard_map/all_gather | solution.py:69
  7.3 192.9 %all-gather.11.cloned.1.call-start = ((), (), s32[]{:S(2)}) async-start(), calls=%async_computation.3 | async-start | bytes 4718592 | tf_op jit(solution)/shard_map/all_gather | solution.py:85
  112.4 180.1 %all-gather.13.cloned.1.call-start = ((), (), s32[]{:S(2)}) async-start(), calls=%async_computation.4 | async-start | bytes 4718592 | tf_op jit(solution)/shard_map/all_gather | solution.py:86
  113.5 716.6 %all-gather.9.cloned.1.call-start = ((), (), s32[]{:S(2)}) async-start(), calls=%async_computation.2 | async-start | bytes 2113536 | tf_op jit(solution)/shard_map/all_gather | solution.py:124
  535.3 298.3 %copy-start.25 = (s32[256,4]{0,1:T(4,128)S(1)}, s32[256,4]{0,1:T(4,128)}, u32[]{:S(2)}) copy-start(s32[256,4]{0,1:T(4,128)} %param.27) | copy-start | bytes 12292
  535.3 298.3 %copy-start.26 = (f32[512]{0:T(512)S(1)}, f32[512]{0:T(512)}, u32[]{:S(2)}) copy-start(f32[512]{0:T(512)} %param.24) | copy-start | bytes 6148
  535.3 298.3 %copy-start.27 = (f32[512]{0:T(512)S(1)}, f32[512]{0:T(512)}, u32[]{:S(2)}) copy-start(f32[512]{0:T(512)} %param.25) | copy-start | bytes 6148
  894.8 7.6 copy-start.16
  894.8 10.4 copy-start.2
  900.4 12.1 copy-start.8
  903.3 11.1 copy-start.5
  994.1 7.6 copy-start.17
  994.1 10.4 copy-start.3
  999.7 12.1 copy-start.9
  1002.5 11.1 copy-start.6
  1093.3 7.6 copy-start.18
  1093.3 10.4 copy-start.4
  1098.9 12.1 copy-start.10
  1101.7 11.1 copy-start.7
  1168.6 11.0 copy-start.21
  1169.9 12.5 %copy-start.24 = (bf16[16,2,32,32]{3,2,1,0:T(8,128)(2,1)S(1)}, bf16[16,2,32,32]{3,2,1,0:T(8,128)(2,1)}, u32[]{:S(2)}) copy-start(bf16[16,2,32,32]{3,2,1,0:T(8,128)(2,1)} %get-tuple-element.530) | copy-start | bytes 196612 | tf_op jit(solution)/shard_map/cond
  1171.1 12.2 copy-start.19
  1173.0 11.2 copy-start.23
  1175.0 10.2 copy-start.22
  1183.6 8.0 copy-start.11
  1185.4 8.9 copy-start.15
  1186.8 9.3 copy-start.14
  1186.8 10.2 copy-start.13
  1189.7 9.2 copy-start.12
  1195.2 7.3 copy-start.30
  1216.9 7.2 copy-start.1
  (3 other events, 9.9 us)
Sparse Core Ops, SparseCore 0:
  9.8 92.5 all-gather.6
  112.6 87.5 all-gather.10
  201.8 90.6 all-gather.12
  530.5 299.5 all-gather.8
where the time goes:
time: 1240 us; the launch traced here: 1230 us
  waiting for transfers between devices  565 us (46%)
  local copies, waits for them, and re-layouts  329 us (27%)
  matrix products  161 us (13%)
  other arithmetic  125 us (10%)
  blocking collectives  31.1 us (3%)
  between operations  17.1 us (1%)
    all_gather x1, waiting for transfers between devices, body(): all_tiles = lax.all_gather(own_tile, ('seq', 'blk'), axis=0, tiled=True)  295 us
    reshape x108, local copies, waits for them, and re-layouts, decode_tile(): tap_list.append(window.reshape(region.shape[0], -1))  96.5 us
    all_gather x1, waiting for transfers between devices, body(): value_piece = lax.all_gather(value_rows, 'blk', axis=0, tiled=True)  92.4 us
    another operation x9, local copies, waits for them, and re-layouts  91 us
    all_gather x1, waiting for transfers between devices, body(): lax.all_gather(tokens, 'seq', axis=0, tiled=True)  90.9 us
    all_gather x1, waiting for transfers between devices, body(): key_piece = lax.all_gather(key_rows, 'blk', axis=0, tiled=True)  86.2 us
    dot_general x8, matrix products, one_block(): jnp.einsum('qhd,khd->hqk', queries, key_block, preferred_element_type=jnp...  72.8 us
    reduce_sum x8, other arithmetic, one_block(): run_sum = run_sum * rescale + jnp.sum(exp_scores, axis=2)  68.4 us
  transfers between devices with their start and end apart: 4, of which 4 were waited for; matrix products, arithmetic and copies ran while one was open for 1% of the time, Pallas kernels for 0%

commit v1 on v0

v1 whole, which is shorter than its diff:
```python
import functools

import jax
import jax.numpy as jnp
import numpy as np
from jax import lax
from jax.experimental import pallas as pl
from jax.experimental.pallas import tpu as pltpu
from jax.sharding import Mesh
from jax.sharding import PartitionSpec as P

HEAD_DIM = 128
LATENT_CH = 16
PATCH = 4
GROUPS = 32
MAXPIX = 4

scale_factor = 0.476986
step_size = 0.25
norm_eps = 1e-06

AXES = ("xh", "z", "c", "y", "xl")
SIZES = (2, 4, 2, 4, 2)
SEQ = ("xh", "z", "c")

NT = (((1,), (1,)), ((), ()))
LOG2E = 1.4426950408889634
PAYLOAD = 80


def shift(x, **moves):
    pairs = []
    for source in range(int(np.prod(SIZES))):
        place = np.unravel_index(source, SIZES)
        target = [(p + moves.get(a, 0)) % n for p, a, n in zip(place, AXES, SIZES)]
        pairs.append((source, int(np.ravel_multi_index(target, SIZES))))
    return lax.ppermute(x, AXES, pairs)


def attention_kernel(bk, nk, xl_ref, q_ref, k_ref, v_ref, w_ref, out_ref, ve_ref):
    @pl.when((pl.program_id(0) == 0) & (pl.program_id(1) == 0))
    def _():
        ve_ref[:, :HEAD_DIM] = v_ref[...]
        ve_ref[:, HEAD_DIM:] = jnp.ones(v_ref.shape, jnp.bfloat16)

    q = q_ref[0]
    bq = q.shape[0]

    def scores_of(i):
        return lax.dot_general(
            q, k_ref[i * bk : (i + 1) * bk, :], NT, preferred_element_type=jnp.float32
        )

    run_max = jnp.full((bq, 1), -1e30, jnp.float32)
    acc = None
    following = scores_of(0)
    for i in range(nk):
        scores = following
        if i + 1 < nk:
            following = scores_of(i + 1)
        new_max = jnp.maximum(run_max, jnp.max(scores, axis=1, keepdims=True))
        probs = jnp.exp2(scores - new_max).astype(jnp.bfloat16)
        part = jnp.dot(probs, ve_ref[i * bk : (i + 1) * bk, :], preferred_element_type=jnp.float32)
        acc = part if acc is None else acc * jnp.exp2(run_max - new_max) + part
        run_max = new_max

    total = acc[:, HEAD_DIM:]
    attended = (acc[:, :HEAD_DIM] / total).astype(jnp.bfloat16)
    velocity = lax.dot_general(w_ref[...], attended, NT, preferred_element_type=jnp.float32)
    log_sum = run_max + jnp.log2(total)
    high = log_sum.astype(jnp.bfloat16)
    rest = log_sum - high.astype(jnp.float32)
    mid = rest.astype(jnp.bfloat16)
    low = (rest - mid.astype(jnp.float32)).astype(jnp.bfloat16)
    lane = lax.broadcasted_iota(jnp.int32, (bq, HEAD_DIM), 1)
    terms = jnp.where(
        lane == 0,
        high.astype(jnp.float32),
        jnp.where(lane == 1, mid.astype(jnp.float32), low.astype(jnp.float32)),
    ).astype(jnp.bfloat16)
    row = lax.broadcasted_iota(jnp.int32, (16, HEAD_DIM), 0)
    column = lax.broadcasted_iota(jnp.int32, (16, HEAD_DIM), 1)
    pick = ((row == column) & (row < 3)).astype(jnp.float32).astype(jnp.bfloat16)
    stats = lax.dot_general(pick, terms, NT, preferred_element_type=jnp.float32)
    joined = jnp.concatenate([velocity, stats], axis=0).astype(jnp.bfloat16)
    for t in range(bq // 128):
        out_ref[t, 0] = joined[:, t * 128 : (t + 1) * 128]


def attention(q, kv, w, my_xl, bq=1024, bk=512):
    rows = q.shape[1]
    length = kv.shape[0]
    blocks = rows // 128
    return pl.pallas_call(
        functools.partial(attention_kernel, bk, length // bk),
        grid_spec=pltpu.PrefetchScalarGridSpec(
            num_scalar_prefetch=1,
            grid=(2, rows // bq),
            in_specs=[
                pl.BlockSpec((1, bq, HEAD_DIM), lambda o, i, xl: (o, i, 0)),
                pl.BlockSpec((length, HEAD_DIM), lambda o, i, xl: (0, 0)),
                pl.BlockSpec((length, HEAD_DIM), lambda o, i, xl: (0, 1)),
                pl.BlockSpec((64, HEAD_DIM), lambda o, i, xl: (0, 0)),
            ],
            out_specs=pl.BlockSpec(
                (bq // 128, 1, PAYLOAD, 128), lambda o, i, xl: (i, (xl[0] + o) % 2, 0, 0)
            ),
            scratch_shapes=[pltpu.VMEM((length, 2 * HEAD_DIM), jnp.bfloat16)],
        ),
        out_shape=jax.ShapeDtypeStruct((blocks, 2, PAYLOAD, 128), jnp.bfloat16),
        compiler_params=pltpu.CompilerParams(vmem_limit_bytes=56 << 20),
        name="attention",
    )(my_xl, q, kv, kv, w)


def combine_kernel(parts_ref, noisy_ref, out_ref):
    velocity = jnp.zeros((64, 128), jnp.float32)
    for head in range(parts_ref.shape[0] // 2):
        logs = []
        for half in range(2):
            terms = parts_ref[2 * head + half, 64:PAYLOAD, :].astype(jnp.float32)
            logs.append(terms[0:1] + terms[1:2] + terms[2:3])
        top = jnp.maximum(logs[0], logs[1])
        first, second = jnp.exp2(logs[0] - top), jnp.exp2(logs[1] - top)
        inverse = 1.0 / (first + second)
        velocity += parts_ref[2 * head, 0:64, :].astype(jnp.float32) * (first * inverse)
        velocity += parts_ref[2 * head + 1, 0:64, :].astype(jnp.float32) * (second * inverse)
    latent = (noisy_ref[...] - step_size * velocity) / scale_factor
    out_ref[...] = latent.astype(jnp.bfloat16)


def combine(parts, noisy):
    return pl.pallas_call(
        combine_kernel,
        out_shape=jax.ShapeDtypeStruct((64, 128), jnp.bfloat16),
        name="latent_tile",
    )(parts, noisy)


def placing_matrix():
    side, p, q, f, i, j = np.meshgrid(*[np.arange(n) for n in (2, 2, 2, 2, 8, 8)], indexing="ij")
    target = f * 512 + (2 * i + p) * 32 + side * 16 + 2 * j + q
    place = np.zeros((1024, 1024), np.float32)
    place[np.arange(1024), target.reshape(-1)] = 1.0
    return place


def decode_kernel(
    ids_ref, tiles_ref, place_ref, first_ref, second_ref, gain_ref, shift_ref, out_ref, wide_ref, half_ref, patch_ref, conv_ref
):
    slot = pl.program_id(0)

    @pl.when(slot == 0)
    def _():
        for s in range(MAXPIX):
            for half in range(2):
                for side in range(2):
                    tile = tiles_ref[ids_ref[1 + s * 4 + half * 2 + side]]
                    for pq in range(4):
                        column = (side * 4 + pq) * 128
                        row = (s * 2 + half) * 16
                        wide_ref[row : row + 16, column : column + 128] = tile[pq * 16 : pq * 16 + 16, :]
        half_ref[...] = jnp.dot(wide_ref[...], place_ref[...], preferred_element_type=jnp.float32)

    @pl.when(slot >= ids_ref[0])
    def _():
        out_ref[...] = jnp.zeros(out_ref.shape, out_ref.dtype)

    @pl.when(slot < ids_ref[0])
    def _():
        start = pl.multiple_of(slot * 32, 32)
        both = half_ref[pl.ds(start, 32), :]
        frames = []
        for f in range(2):
            frames.append(
                jnp.concatenate(
                    [both[0:16, f * 512 : f * 512 + 512], both[16:32, f * 512 : f * 512 + 512]], axis=1
                )
            )
        region = jnp.concatenate(frames, axis=0)
        lane = lax.broadcasted_iota(jnp.int32, region.shape, 1)
        column = lane % 32
        for g in range(3):
            if g == 0:
                across = jnp.where(column == 0, region, pltpu.roll(region, 1, 1))
            elif g == 1:
                across = region
            else:
                across = jnp.where(column == 31, region, pltpu.roll(region, 1023, 1))
            for b in range(3):
                if b == 0:
                    tap = jnp.where(lane < 32, across, pltpu.roll(across, 32, 1))
                elif b == 1:
                    tap = across
                else:
                    tap = jnp.where(lane >= 992, across, pltpu.roll(across, 992, 1))
                row = (b * 3 + g) * 16
                tap = tap.astype(jnp.bfloat16)
                patch_ref[row : row + 16, :] = tap[0:16]
                patch_ref[144 + row : 144 + row + 16, :] = tap[16:32]
        conv_ref[:, :1024] = jnp.dot(
            first_ref[...], patch_ref[0:144, :], preferred_element_type=jnp.float32
        )
        conv_ref[:, 1024:] = jnp.dot(
            second_ref[...], patch_ref[...], preferred_element_type=jnp.float32
        )
        size = conv_ref.shape[0] // GROUPS
        count = 1.0 / (size * conv_ref.shape[1])
        for group in range(GROUPS):
            rows = slice(group * size, (group + 1) * size)
            values = conv_ref[rows, :]
            mean = jnp.sum(jnp.sum(values, axis=0, keepdims=True), axis=1, keepdims=True) * count
            apart = values - mean
            squares = apart * apart
            var = jnp.sum(jnp.sum(squares, axis=0, keepdims=True), axis=1, keepdims=True) * count
            scale = gain_ref[rows, :] * lax.rsqrt(var + norm_eps) * 0.5
            half_norm = apart * scale + shift_ref[rows, :] * 0.5
            out_ref[0, 0, rows, :] = (half_norm + half_norm * jnp.tanh(half_norm)).astype(jnp.bfloat16)


def decode(ids, tiles, place, first, second, gain, shift_rows):
    channels = first.shape[0]
    whole = lambda shape: pl.BlockSpec(shape, lambda s, ids: (0,) * len(shape))
    return pl.pallas_call(
        decode_kernel,
        grid_spec=pltpu.PrefetchScalarGridSpec(
            num_scalar_prefetch=1,
            grid=(MAXPIX,),
            in_specs=[
                whole(tiles.shape),
                whole(place.shape),
                whole(first.shape),
                whole(second.shape),
                whole(gain.shape),
                whole(shift_rows.shape),
            ],
            out_specs=pl.BlockSpec((1, 1, channels, 2048), lambda s, ids: (0, s, 0, 0)),
            scratch_shapes=[
                pltpu.VMEM((128, 1024), jnp.bfloat16),
                pltpu.VMEM((128, 1024), jnp.float32),
                pltpu.VMEM((288, 1024), jnp.bfloat16),
                pltpu.VMEM((channels, 2048), jnp.float32),
            ],
        ),
        out_shape=jax.ShapeDtypeStruct((1, MAXPIX, channels, 2048), jnp.bfloat16),
        compiler_params=pltpu.CompilerParams(vmem_limit_bytes=56 << 20),
        name="decode",
    )(ids, tiles, place, first, second, gain, shift_rows)


def body(
    tokens,
    project_weight,
    noisy_latent,
    final_weight,
    conv_weight,
    norm_gain,
    norm_shift,
    owner_count,
    intersection,
):
    my_xl = lax.axis_index("xl")
    head = lax.axis_index(SEQ)

    gathered = lax.all_gather(tokens, SEQ, axis=0, tiled=True)
    own_q = jnp.dot(gathered, project_weight[0], preferred_element_type=jnp.float32)
    own_q = (own_q * (LOG2E * HEAD_DIM**-0.5)).astype(jnp.bfloat16)
    own_kv = jnp.dot(
        gathered,
        jnp.concatenate([project_weight[1], project_weight[2]], axis=1),
        preferred_element_type=jnp.float32,
    ).astype(jnp.bfloat16)
    queries = jnp.stack([own_q, shift(own_q, xl=1)])
    kv = lax.all_gather(own_kv, "y", axis=0, tiled=True)

    w = lax.dynamic_slice_in_dim(final_weight, head * HEAD_DIM, HEAD_DIM, axis=0)
    w = w.reshape(HEAD_DIM, LATENT_CH, PATCH).transpose(2, 1, 0).reshape(64, HEAD_DIM)
    noisy = noisy_latent.reshape(-1, LATENT_CH, PATCH).transpose(2, 1, 0).reshape(64, -1)

    parts = attention(queries, kv, w, my_xl.astype(jnp.int32).reshape(1))
    parts = parts.reshape(-1, PAYLOAD, 128)
    parts = lax.all_to_all(parts, SEQ + ("xl",), split_axis=0, concat_axis=0, tiled=True)
    tile = combine(parts, noisy)

    tiles = lax.all_to_all(
        jnp.broadcast_to(tile[None], (128,) + tile.shape), AXES, split_axis=0, concat_axis=0, tiled=True
    )

    rank = lax.axis_index(AXES)
    ends = jnp.cumsum(owner_count, dtype=jnp.int32)
    count = owner_count[rank]
    slots = jnp.minimum(ends[rank] - count + jnp.arange(MAXPIX), intersection.shape[0] - 1)
    ids = jnp.concatenate([count[None], intersection[slots].reshape(-1)]).astype(jnp.int32)

    taps = conv_weight.astype(jnp.float32).reshape(3, -1, conv_weight.shape[1])
    first = (taps[0] + taps[1] + taps[2]).T.astype(jnp.bfloat16)
    second = jnp.concatenate([taps[0] + taps[1], taps[2]], axis=0).T.astype(jnp.bfloat16)
    place = jnp.asarray(placing_matrix(), jnp.bfloat16)
    return decode(ids, tiles, place, first, second, norm_gain[:, None], norm_shift[:, None])


def solution(mesh):
    fine = Mesh(mesh.devices.reshape(SIZES), AXES)
    blk = ("y", "xl")
    return jax.shard_map(
        body,
        mesh=fine,
        in_specs=(
            P(SEQ + blk, None),
            P(None, None, SEQ),
            P(SEQ + blk, None),
            P(),
            P(),
            P(),
            P(),
            P(),
            P(),
        ),
        out_specs=P(SEQ + blk, None, None, None),
        check_vma=False,
    )
```

time: 1240 us -> 282 us (0.23)
  the two profiles are of different devices: /device:TPU:19 before, /device:TPU:9 now
where the time goes in v1:
time: 282 us; the launch traced here: 281 us
  waiting for transfers between devices  155 us (55%)
  Pallas kernels  58.9 us (21%)
  local copies, waits for them, and re-layouts  15.7 us (6%)
  matrix products  15.6 us (6%)
  between operations  14.8 us (5%)
  starting transfers between devices  14.7 us (5%)
  other arithmetic  6.53 us (2%)
    all_gather x1, waiting for transfers between devices, body(): gathered = lax.all_gather(tokens, SEQ, axis=0, tiled=True)  94.7 us
    pallas_call x1, Pallas kernels, attention(): pl.pallas_call(functools.partial(attention_kernel, bk, length // bk), gri...  42.5 us
    all_gather x1, waiting for transfers between devices, body(): kv = lax.all_gather(own_kv, 'y', axis=0, tiled=True)  22.1 us
    pallas_call x1, Pallas kernels, decode(): pl.pallas_call(decode_kernel, grid_spec=pltpu.PrefetchScalarGridSpec(num_...  14.4 us
    all_to_all x1, waiting for transfers between devices, body(): lax.all_to_all(jnp.broadcast_to(tile[None], (128,) + tile.shape), AXES, s...  13.6 us
    ppermute x1, waiting for transfers between devices, shift(): return lax.ppermute(x, AXES, pairs)  12.5 us
    all_to_all x1, waiting for transfers between devices, body(): lax.all_to_all(parts, SEQ + ('xl',), split_axis=0, concat_axis=0, tiled=T...  11.4 us
    dot_general x1, matrix products, body(): jnp.dot(gathered, project_weight[0], preferred_element_type=jnp.float32)  8.15 us
  transfers between devices with their start and end apart: 5, of which 5 were waited for; matrix products, arithmetic and copies ran while one was open for 9% of the time, Pallas kernels for 0%

profile of v1, /device:TPU:9, one launch (start us, length us, event | category | flops | bytes accessed | tf_op | source)
XLA Modules:
  0.0 281.3 jit_solution(11079912081613148198)
XLA Ops:
  6.5 0.7 all-gather.3.cloned.1.call-update
  7.3 1.5 slice_bitcast_fusion.1
  8.8 94.7 %all-gather.3.cloned.1.call-done = bf16[2048,3072]{1,0:T(8,128)(2,1)} async-done(((bf16[128,3072]{1,0:T(8,128)(2,1)}), bf16[2048,3072]{1,0:T(8,128)(2,1)}) %all-gather.3.cloned.1.call-update) | async-done | bytes 12582928 | tf_op jit(solution)/shard_map/all_gather | solution.py:265
  103.5 7.5 %fusion = bf16[2048,256]{1,0:T(8,128)(2,1)} fusion(bf16[2048,3072]{1,0:T(8,128)(2,1)} %all-gather.3.cloned.1.call-done, bf16[3072,128]{1,0:T(8,128)(2,1)S(1)} %get-tuple-element.6, bf16[3072,128]{1,0:T(8,128)(2,1)S(1)} %get-tuple-element.5), kind=kOutput, calls=%fused_computation.2 | convolution fusion | flops 3224895488 | bytes 15204352 | tf_op jit(solution)/shard_map/dot_general | solution.py:268
  111.0 8.2 %fusion.1 = bf16[2048,128]{1,0:T(8,128)(2,1)S(1)} fusion(bf16[2048,3072]{1,0:T(8,128)(2,1)} %all-gather.3.cloned.1.call-done, bf16[3,3072,128]{2,1,0:T(8,128)(2,1)} %param.11), kind=kOutput, calls=%fused_computation.4 | convolution fusion | flops 1611137024 | bytes 13893632 | tf_op jit(solution)/shard_map/dot_general | solution.py:266
  119.7 0.6 copy.19
  120.3 12.5 %collective-permute-done = bf16[2048,128]{1,0:T(8,128)(2,1)S(1)} collective-permute-done((bf16[2048,128]{1,0:T(8,128)(2,1)S(1)}, bf16[2048,128]{1,0:T(8,128)(2,1)S(1)}, u32[]{:S(2)}, u32[]{:S(2)}) %collective-permute-start) | collective-permute-done | bytes 524320 | tf_op jit(solution)/shard_map/ppermute | solution.py:37
  132.8 1.1 pad_maximum_fusion.q_ref
  133.8 22.1 %all-gather.5.cloned.1.call-done.k_ref.v_ref = bf16[8192,256]{1,0:T(8,128)(2,1)} async-done(((bf16[2048,256]{1,0:T(8,128)(2,1)}), bf16[8192,256]{1,0:T(8,128)(2,1)}) %all-gather.5.cloned.1.call-update) | async-done | bytes 4194320 | tf_op jit(solution)/shard_map/all_gather | solution.py:274
  156.0 42.5 %attention.1 = bf16[16,2,80,128]{3,2,1,0:T(8,128)(2,1)} custom-call(s32[1]{0:T(128)} %bitcast.4.xl_ref, bf16[2,2048,128]{2,1,0:T(8,128)(2,1)} %pad_maximum_fusion.q_ref, bf16[8192,256]{1,0:T(8,128)(2,1)} %all-gather.5.cloned.1.call-done.k_ref.v_ref, bf16[8192,256]{1,0:T(8,128)(2,1)} %all-gather.5.cloned.1.call-done.k_ref.v_ref, bf16[64,128]{1,0:T(8,128)(2,1)} %bitcast.38), custom_call_target="tpu_custom_call" | custom-call | tf_op jit(solution)/shard_map/attention/pallas_call | solution.py:94
  198.5 7.7 %all-to-all-start = ((bf16[32,80,128]{2,1,0:T(8,128)(2,1)}), bf16[32,80,128]{2,1,0:T(8,128)(2,1)S(1)}, u32[]{:S(2)}, u32[]{:S(2)}) async-start(bf16[32,80,128]{2,1,0:T(8,128)(2,1)} %bitcast.34), calls=%async_computation | async-start | bytes 1310720 | tf_op jit(solution)/shard_map/all_to_all | solution.py:282
  206.2 0.6 copy.20
  206.8 11.4 %all-to-all-done.parts_ref = bf16[32,80,128]{2,1,0:T(8,128)(2,1)S(1)} async-done(((bf16[32,80,128]{2,1,0:T(8,128)(2,1)}), bf16[32,80,128]{2,1,0:T(8,128)(2,1)S(1)}, u32[]{:S(2)}, u32[]{:S(2)}) %all-to-all-start) | async-done | bytes 655392 | tf_op jit(solution)/shard_map/all_to_all | solution.py:282
  218.3 0.8 copy-done.2
  219.1 1.9 latent_tile.1
  221.0 2.6 broadcast_in_dim.6
  223.6 6.4 %all-to-all-start.1 = ((bf16[128,64,128]{2,1,0:T(8,128)(2,1)}), bf16[128,64,128]{2,1,0:T(8,128)(2,1)S(1)}, u32[]{:S(2)}, u32[]{:S(2)}) async-start(bf16[128,64,128]{2,1,0:T(8,128)(2,1)} %broadcast_in_dim.6), calls=%async_computation.1 | async-start | bytes 4194304 | tf_op jit(solution)/shard_map/all_to_all | solution.py:285
  230.1 1.0 copy.21
  231.1 1.2 convert_element_type.23
  232.2 1.8 slice.55
  234.0 0.8 copy.17
  235.1 0.6 dynamic_slice.9
  235.8 0.6 constant_dynamic-slice_fusion.1
  237.7 1.5 gather_fusion
  239.2 0.9 copy.22.gain_ref
  240.1 0.9 copy.23.shift_ref
  241.0 1.2 pad_add_fusion.ids_ref
  242.2 1.1 fusion.8
  243.2 1.8 maximum_bitcast_fusion.second_ref
  245.1 13.6 %all-to-all-done.1.tiles_ref = bf16[128,64,128]{2,1,0:T(8,128)(2,1)S(1)} async-done(((bf16[128,64,128]{2,1,0:T(8,128)(2,1)}), bf16[128,64,128]{2,1,0:T(8,128)(2,1)S(1)}, u32[]{:S(2)}, u32[]{:S(2)}) %all-to-all-start.1) | async-done | bytes 2097184 | tf_op jit(solution)/shard_map/all_to_all | solution.py:285
  258.7 1.3 copy-done.1
  260.0 14.4 %decode.1 = bf16[1,4,512,2048]{3,2,1,0:T(8,128)(2,1)} custom-call(s32[17]{0:T(128)} %pad_add_fusion.ids_ref, bf16[128,64,128]{2,1,0:T(8,128)(2,1)} %copy-done.1, bf16[1024,1024]{1,0:T(8,128)(2,1)} %constant.46.clone.place_ref, bf16[512,144]{1,0:T(8,128)(2,1)} %get-tuple-element.8.first_ref, bf16[512,288]{1,0:T(8,128)(2,1)} %maximum_bitcast_fusion.second_ref, ...), custom_call_target="tpu_custom_call" | custom-call | tf_op jit(solution)/shard_map/decode/pallas_call | solution.py:224
  (26 shorter events, 1.0 us)
Async XLA Ops:
  6.5 113.2 %copy-start = (bf16[2048,64]{0,1:T(8,128)(2,1)S(1)}, bf16[2048,64]{0,1:T(8,128)(2,1)}, u32[]{:S(2)}) copy-start(bf16[2048,64]{0,1:T(8,128)(2,1)} %param.13) | copy-start | bytes 786436
  6.5 97.0 %all-gather.3.cloned.1.call-start = ((), (), s32[]{:S(2)}) async-start(), calls=%async_computation.2 | async-start | bytes 13369344 | tf_op jit(solution)/shard_map/all_gather | solution.py:265
  7.3 148.7 %all-gather.5.cloned.1.call-start = ((), (), s32[]{:S(2)}) async-start(), calls=%async_computation.3 | async-start | bytes 5242880 | tf_op jit(solution)/shard_map/all_gather | solution.py:274
  119.1 13.6 %collective-permute-start = (bf16[2048,128]{1,0:T(8,128)(2,1)S(1)}, bf16[2048,128]{1,0:T(8,128)(2,1)S(1)}, u32[]{:S(2)}, u32[]{:S(2)}) collective-permute-start(bf16[2048,128]{1,0:T(8,128)(2,1)S(1)} %fusion.1), channel_id=1, source_target_pairs={{0,1},{1,0},{2,3},{3,2},{4,5},{5,4},{6,7},{7,6},{8,9},{9,8},{10,11... | collective-permute-start | bytes 1572872 | tf_op jit(solution)/shard_map/ppermute | solution.py:37
  156.0 50.2 %copy-start.4 = (f32[128,64]{0,1:T(8,128)S(1)}, f32[128,64]{0,1:T(8,128)}, u32[]{:S(2)}) copy-start(f32[128,64]{0,1:T(8,128)} %param.12) | copy-start | bytes 98308
  198.5 19.7 %all-to-all-start = ((bf16[32,80,128]{2,1,0:T(8,128)(2,1)}), bf16[32,80,128]{2,1,0:T(8,128)(2,1)S(1)}, u32[]{:S(2)}, u32[]{:S(2)}) async-start(bf16[32,80,128]{2,1,0:T(8,128)(2,1)} %bitcast.34), calls=%async_computation | async-start | bytes 1310720 | tf_op jit(solution)/shard_map/all_to_all | solution.py:282
  218.3 0.8 copy-start.2
  221.0 9.0 %copy-start.3 = (bf16[432,512]{1,0:T(8,128)(2,1)S(1)}, bf16[432,512]{1,0:T(8,128)(2,1)}, u32[]{:S(2)}) copy-start(bf16[432,512]{1,0:T(8,128)(2,1)} %param.14) | copy-start | bytes 1327108
  223.6 10.4 %copy-start.5 = (s32[256,4]{0,1:T(4,128)S(1)}, s32[256,4]{0,1:T(4,128)}, u32[]{:S(2)}) copy-start(s32[256,4]{0,1:T(4,128)} %param.18) | copy-start | bytes 12292
  223.6 11.2 %copy-start.8 = (s32[128]{0:T(128)S(1)}, s32[128]{0:T(128)}, u32[]{:S(2)}) copy-start(s32[128]{0:T(128)} %param.17) | copy-start | bytes 1540
  223.6 15.6 %copy-start.6 = (f32[512]{0:T(512)S(1)}, f32[512]{0:T(512)}, u32[]{:S(2)}) copy-start(f32[512]{0:T(512)} %param.15) | copy-start | bytes 6148
  223.6 16.5 %copy-start.7 = (f32[512]{0:T(512)S(1)}, f32[512]{0:T(512)}, u32[]{:S(2)}) copy-start(f32[512]{0:T(512)} %param.16) | copy-start | bytes 6148
  223.6 35.0 %all-to-all-start.1 = ((bf16[128,64,128]{2,1,0:T(8,128)(2,1)}), bf16[128,64,128]{2,1,0:T(8,128)(2,1)S(1)}, u32[]{:S(2)}, u32[]{:S(2)}) async-start(bf16[128,64,128]{2,1,0:T(8,128)(2,1)} %broadcast_in_dim.6), calls=%async_computation.1 | async-start | bytes 4194304 | tf_op jit(solution)/shard_map/all_to_all | solution.py:285
  258.7 1.3 copy-start.1
Sparse Core Ops, SparseCore 0:
  9.8 93.6 all-gather.2
  111.1 44.8 all-gather.4

commit v2 on v1

--- a/solution.py
+++ b/solution.py
@@ -37,80 +37,182 @@
     return lax.ppermute(x, AXES, pairs)
 
 
-def attention_kernel(bk, nk, xl_ref, q_ref, k_ref, v_ref, w_ref, out_ref, ve_ref):
-    @pl.when((pl.program_id(0) == 0) & (pl.program_id(1) == 0))
-    def _():
-        ve_ref[:, :HEAD_DIM] = v_ref[...]
-        ve_ref[:, HEAD_DIM:] = jnp.ones(v_ref.shape, jnp.bfloat16)
-
-    q = q_ref[0]
-    bq = q.shape[0]
-
-    def scores_of(i):
+def project_kernel(steps, scale, n_after, *refs):
+    x_refs, refs = refs[: len(steps)], refs[len(steps) :]
+    w_ref, out_refs = refs[0], refs[1 + n_after :]
+    step = pl.program_id(0)
+    start = 0
+    for x_ref, count in zip(x_refs, steps):
+
+        def multiply(x_ref=x_ref):
+            out = jnp.dot(x_ref[...], w_ref[...], preferred_element_type=jnp.float32)
+            column = 0
+            for n, out_ref in enumerate(out_refs):
+                width = out_ref.shape[1]
+                part = out[:, column : column + width]
+                out_ref[...] = (part * scale if n % 2 == 0 else part).astype(jnp.bfloat16)
+                column += width
+
+        pl.when((step >= start) & (step < start + count))(multiply)
+        start += count
+
+
+def project(xs, w, scale, after=(), bm=256):
+    steps = [x.shape[0] // bm for x in xs]
+    starts = np.cumsum([0] + steps)
+    rows = int(starts[-1]) * bm
+    widths = [HEAD_DIM, 2 * HEAD_DIM] * 2
+    in_specs = [
+        pl.BlockSpec((bm, x.shape[1]), lambda i, a=int(a), n=n: (jnp.clip(i - a, 0, n - 1), 0))
+        for x, a, n in zip(xs, starts, steps)
+    ]
+    in_specs.append(pl.BlockSpec(w.shape, lambda i: (0, 0)))
+    in_specs += [pl.BlockSpec(memory_space=pl.ANY)] * len(after)
+    return pl.pallas_call(
+        functools.partial(project_kernel, steps, scale, len(after)),
+        grid=(rows // bm,),
+        in_specs=in_specs,
+        out_specs=[pl.BlockSpec((bm, width), lambda i: (i, 0)) for width in widths],
+        out_shape=[jax.ShapeDtypeStruct((rows, width), jnp.bfloat16) for width in widths],
+        compiler_params=pltpu.CompilerParams(vmem_limit_bytes=56 << 20),
+        name="project",
+    )(*xs, w, *after)
+
+
+def softmax_blocks(q, kv_refs, value_ref, bk, run_max, acc):
+    places, start = [], 0
+    for ref in kv_refs:
+        for i in range(0, ref.shape[0], bk):
+            places.append((ref, i, start + i))
+        start += ref.shape[0]
+
+    def scores_of(n):
+        ref, i, _ = places[n]
         return lax.dot_general(
-            q, k_ref[i * bk : (i + 1) * bk, :], NT, preferred_element_type=jnp.float32
+            q, ref[i : i + bk, :HEAD_DIM], NT, preferred_element_type=jnp.float32
         )
 
-    run_max = jnp.full((bq, 1), -1e30, jnp.float32)
-    acc = None
     following = scores_of(0)
-    for i in range(nk):
+    for n, (_, _, row) in enumerate(places):
         scores = following
-        if i + 1 < nk:
-            following = scores_of(i + 1)
-        new_max = jnp.maximum(run_max, jnp.max(scores, axis=1, keepdims=True))
+        if n + 1 < len(places):
+            following = scores_of(n + 1)
+        new_max = jnp.max(scores, axis=1, keepdims=True)
+        if run_max is not None:
+            new_max = jnp.maximum(run_max, new_max)
         probs = jnp.exp2(scores - new_max).astype(jnp.bfloat16)
-        part = jnp.dot(probs, ve_ref[i * bk : (i + 1) * bk, :], preferred_element_type=jnp.float32)
+        part = jnp.dot(probs, value_ref[row : row + bk, :], preferred_element_type=jnp.float32)
         acc = part if acc is None else acc * jnp.exp2(run_max - new_max) + part
         run_max = new_max
+    return run_max, acc
+
+
+def attention_kernel(bk, n_kv, carry_in, n_into, final, *refs):
+    if final:
+        place_ref, *refs = refs
+    q_ref, *refs = refs
+    kv_refs, refs = refs[:n_kv], refs[n_kv:]
+    if carry_in:
+        acc_in_ref, max_in_ref, *refs = refs
+    refs = refs[n_into:]
+    if final:
+        w_ref, out_ref, value_ref = refs
+    else:
+        acc_out_ref, max_out_ref, value_ref = refs
+
+    @pl.when(pl.program_id(0) == 0)
+    def _():
+        start = 0
+        for ref in kv_refs:
+            n = ref.shape[0]
+            value_ref[start : start + n, :HEAD_DIM] = ref[:, HEAD_DIM:]
+            value_ref[start : start + n, HEAD_DIM:] = jnp.ones((n, HEAD_DIM), jnp.bfloat16)
+            start += n
+
+    q = q_ref[...]
+    bq = q.shape[0]
+    run_max, acc = None, None
+    if carry_in:
+        run_max, acc = jnp.max(max_in_ref[...], axis=1, keepdims=True), acc_in_ref[...]
+    run_max, acc = softmax_blocks(q, kv_refs, value_ref, bk, run_max, acc)
+    if not final:
+        acc_out_ref[...] = acc
+        max_out_ref[...] = jnp.broadcast_to(run_max, max_out_ref.shape)
+        return
 
     total = acc[:, HEAD_DIM:]
     attended = (acc[:, :HEAD_DIM] / total).astype(jnp.bfloat16)
     velocity = lax.dot_general(w_ref[...], attended, NT, preferred_element_type=jnp.float32)
     log_sum = run_max + jnp.log2(total)
-    high = log_sum.astype(jnp.bfloat16)
-    rest = log_sum - high.astype(jnp.float32)
-    mid = rest.astype(jnp.bfloat16)
-    low = (rest - mid.astype(jnp.float32)).astype(jnp.bfloat16)
+    high = log_sum.astype(jnp.bfloat16).astype(jnp.float32)
+    mid = (log_sum - high).astype(jnp.bfloat16).astype(jnp.float32)
+    low = log_sum - high - mid
     lane = lax.broadcasted_iota(jnp.int32, (bq, HEAD_DIM), 1)
-    terms = jnp.where(
-        lane == 0,
-        high.astype(jnp.float32),
-        jnp.where(lane == 1, mid.astype(jnp.float32), low.astype(jnp.float32)),
-    ).astype(jnp.bfloat16)
-    row = lax.broadcasted_iota(jnp.int32, (16, HEAD_DIM), 0)
-    column = lax.broadcasted_iota(jnp.int32, (16, HEAD_DIM), 1)
+    terms = jnp.where(lane == 0, high, jnp.where(lane == 1, mid, low)).astype(jnp.bfloat16)
+    row = lax.broadcasted_iota(jnp.int32, (PAYLOAD - 64, HEAD_DIM), 0)
+    column = lax.broadcasted_iota(jnp.int32, (PAYLOAD - 64, HEAD_DIM), 1)
     pick = ((row == column) & (row < 3)).astype(jnp.float32).astype(jnp.bfloat16)
     stats = lax.dot_general(pick, terms, NT, preferred_element_type=jnp.float32)
     joined = jnp.concatenate([velocity, stats], axis=0).astype(jnp.bfloat16)
-    for t in range(bq // 128):
-        out_ref[t, 0] = joined[:, t * 128 : (t + 1) * 128]
-
-
-def attention(q, kv, w, my_xl, bq=1024, bk=512):
-    rows = q.shape[1]
-    length = kv.shape[0]
-    blocks = rows // 128
+    cores, depth = out_ref.shape[2], out_ref.shape[1]
+    for core in range(cores):
+        for z in range(depth):
+            t = core * depth + z
+            out_ref[0, z, (core + place_ref[2]) % cores, 0] = joined[:, t * 128 : (t + 1) * 128]
+
+
+def attention(q, kvs, carry=None, into=None, rows_out=None, last=None, bq=1024, bk=512):
+    rows = q.shape[0]
+    rows_out = rows_out or rows
+    skip = 0
+    length = sum(kv.shape[0] for kv in kvs)
+    by_row = lambda width: pl.BlockSpec((bq, width), lambda i, *p: (i, 0))
+    whole = lambda x: pl.BlockSpec(x.shape, lambda i, *p: (0, 0))
+    operands, in_specs = [q, *kvs], [by_row(HEAD_DIM)] + [whole(kv) for kv in kvs]
+    if carry is not None:
+        operands += carry
+        in_specs += [by_row(2 * HEAD_DIM), by_row(HEAD_DIM)]
+    aliases = {}
+    if into is not None:
+        aliases = {len(operands): 0, len(operands) + 1: 1}
+        operands += into
+        in_specs += [pl.BlockSpec(memory_space=pl.ANY)] * 2
+        rows_out = into[0].shape[0]
+        skip = (rows_out - rows) // bq
+    if last is None:
+        prefetch = []
+        out_specs = [
+            pl.BlockSpec((bq, width), lambda i: (i + skip, 0)) for width in (2 * HEAD_DIM, HEAD_DIM)
+        ]
+        out_shape = [
+            jax.ShapeDtypeStruct((rows_out, 2 * HEAD_DIM), jnp.float32),
+            jax.ShapeDtypeStruct((rows_out, HEAD_DIM), jnp.float32),
+        ]
+    else:
+        prefetch = [last[0]]
+        operands.append(last[1])
+        in_specs.append(whole(last[1]))
+        out_specs = pl.BlockSpec(
+            (1, 4, 2, 1, PAYLOAD, 128),
+            lambda i, p: ((i % 2 + p[1]) % 2, 0, 0, (i // 2 + p[0]) % 2, 0, 0),
+        )
+        out_shape = jax.ShapeDtypeStruct((2, 4, 2, 2, PAYLOAD, 128), jnp.bfloat16)
     return pl.pallas_call(
-        functools.partial(attention_kernel, bk, length // bk),
+        functools.partial(
+            attention_kernel, bk, len(kvs), carry is not None, len(aliases), last is not None
+        ),
         grid_spec=pltpu.PrefetchScalarGridSpec(
-            num_scalar_prefetch=1,
-            grid=(2, rows // bq),
-            in_specs=[
-                pl.BlockSpec((1, bq, HEAD_DIM), lambda o, i, xl: (o, i, 0)),
-                pl.BlockSpec((length, HEAD_DIM), lambda o, i, xl: (0, 0)),
-                pl.BlockSpec((length, HEAD_DIM), lambda o, i, xl: (0, 1)),
-                pl.BlockSpec((64, HEAD_DIM), lambda o, i, xl: (0, 0)),
-            ],
-            out_specs=pl.BlockSpec(
-                (bq // 128, 1, PAYLOAD, 128), lambda o, i, xl: (i, (xl[0] + o) % 2, 0, 0)
-            ),
+            num_scalar_prefetch=len(prefetch),
+            grid=(rows // bq,),
+            in_specs=in_specs,
+            out_specs=out_specs,
             scratch_shapes=[pltpu.VMEM((length, 2 * HEAD_DIM), jnp.bfloat16)],
         ),
-        out_shape=jax.ShapeDtypeStruct((blocks, 2, PAYLOAD, 128), jnp.bfloat16),
+        out_shape=out_shape,
+        input_output_aliases=aliases,
         compiler_params=pltpu.CompilerParams(vmem_limit_bytes=56 << 20),
         name="attention",
-    )(my_xl, q, kv, kv, w)
+    )(*prefetch, *operands)
 
 
 def combine_kernel(parts_ref, noisy_ref, out_ref):
@@ -126,13 +228,15 @@
         velocity += parts_ref[2 * head, 0:64, :].astype(jnp.float32) * (first * inverse)
         velocity += parts_ref[2 * head + 1, 0:64, :].astype(jnp.float32) * (second * inverse)
     latent = (noisy_ref[...] - step_size * velocity) / scale_factor
-    out_ref[...] = latent.astype(jnp.bfloat16)
-
-
-def combine(parts, noisy):
+    latent = latent.astype(jnp.bfloat16)
+    for n in range(out_ref.shape[0]):
+        out_ref[n] = latent
+
+
+def combine(parts, noisy, copies):
     return pl.pallas_call(
         combine_kernel,
-        out_shape=jax.ShapeDtypeStruct((64, 128), jnp.bfloat16),
+        out_shape=jax.ShapeDtypeStruct((copies, 64, 128), jnp.bfloat16),
         name="latent_tile",
     )(parts, noisy)
 
@@ -146,7 +250,7 @@
 
 
 def decode_kernel(
-    ids_ref, tiles_ref, place_ref, first_ref, second_ref, gain_ref, shift_ref, out_ref, wide_ref, half_ref, patch_ref, conv_ref
+    ids_ref, own_ref, other_ref, place_ref, first_ref, second_ref, gain_ref, shift_ref, out_ref, wide_ref, half_ref, patch_ref, conv_ref
 ):
     slot = pl.program_id(0)
 
@@ -155,7 +259,8 @@
         for s in range(MAXPIX):
             for half in range(2):
                 for side in range(2):
-                    tile = tiles_ref[ids_ref[1 + s * 4 + half * 2 + side]]
+                    n = ids_ref[1 + s * 4 + half * 2 + side]
+                    tile = jnp.where(n < 64, own_ref[n % 64], other_ref[n % 64])
                     for pq in range(4):
                         column = (side * 4 + pq) * 128
                         row = (s * 2 + half) * 16
@@ -218,7 +323,7 @@
             out_ref[0, 0, rows, :] = (half_norm + half_norm * jnp.tanh(half_norm)).astype(jnp.bfloat16)
 
 
-def decode(ids, tiles, place, first, second, gain, shift_rows):
+def decode(ids, own_tiles, other_tiles, place, first, second, gain, shift_rows):
     channels = first.shape[0]
     whole = lambda shape: pl.BlockSpec(shape, lambda s, ids: (0,) * len(shape))
     return pl.pallas_call(
@@ -227,7 +332,8 @@
             num_scalar_prefetch=1,
             grid=(MAXPIX,),
             in_specs=[
-                whole(tiles.shape),
+                whole(own_tiles.shape),
+                whole(other_tiles.shape),
                 whole(place.shape),
                 whole(first.shape),
                 whole(second.shape),
@@ -245,7 +351,7 @@
         out_shape=jax.ShapeDtypeStruct((1, MAXPIX, channels, 2048), jnp.bfloat16),
         compiler_params=pltpu.CompilerParams(vmem_limit_bytes=56 << 20),
         name="decode",
-    )(ids, tiles, place, first, second, gain, shift_rows)
+    )(ids, own_tiles, other_tiles, place, first, second, gain, shift_rows)
 
 
 def body(
@@ -259,44 +365,71 @@
     owner_count,
     intersection,
 ):
-    my_xl = lax.axis_index("xl")
+    coordinate = {axis: lax.axis_index(axis).astype(jnp.int32) for axis in AXES}
     head = lax.axis_index(SEQ)
 
-    gathered = lax.all_gather(tokens, SEQ, axis=0, tiled=True)
-    own_q = jnp.dot(gathered, project_weight[0], preferred_element_type=jnp.float32)
-    own_q = (own_q * (LOG2E * HEAD_DIM**-0.5)).astype(jnp.bfloat16)
-    own_kv = jnp.dot(
-        gathered,
-        jnp.concatenate([project_weight[1], project_weight[2]], axis=1),
-        preferred_element_type=jnp.float32,
-    ).astype(jnp.bfloat16)
-    queries = jnp.stack([own_q, shift(own_q, xl=1)])
-    kv = lax.all_gather(own_kv, "y", axis=0, tiled=True)
+    weights = jnp.concatenate([project_weight, shift(project_weight, c=1)])
+    weights = weights.transpose(1, 0, 2).reshape(weights.shape[1], -1)
 
     w = lax.dynamic_slice_in_dim(final_weight, head * HEAD_DIM, HEAD_DIM, axis=0)
     w = w.reshape(HEAD_DIM, LATENT_CH, PATCH).transpose(2, 1, 0).reshape(64, HEAD_DIM)
     noisy = noisy_latent.reshape(-1, LATENT_CH, PATCH).transpose(2, 1, 0).reshape(64, -1)
-
-    parts = attention(queries, kv, w, my_xl.astype(jnp.int32).reshape(1))
-    parts = parts.reshape(-1, PAYLOAD, 128)
-    parts = lax.all_to_all(parts, SEQ + ("xl",), split_axis=0, concat_axis=0, tiled=True)
-    tile = combine(parts, noisy)
-
-    tiles = lax.all_to_all(
-        jnp.broadcast_to(tile[None], (128,) + tile.shape), AXES, split_axis=0, concat_axis=0, tiled=True
-    )
 
     rank = lax.axis_index(AXES)
     ends = jnp.cumsum(owner_count, dtype=jnp.int32)
     count = owner_count[rank]
     slots = jnp.minimum(ends[rank] - count + jnp.arange(MAXPIX), intersection.shape[0] - 1)
-    ids = jnp.concatenate([count[None], intersection[slots].reshape(-1)]).astype(jnp.int32)
+    wanted = intersection[slots].reshape(-1)
+    core = (wanted // 8) % 2
+    wanted = (wanted // 16) * 8 + wanted % 8 + 64 * (core != coordinate["c"])
+    ids = jnp.concatenate([count[None], wanted]).astype(jnp.int32)
 
     taps = conv_weight.astype(jnp.float32).reshape(3, -1, conv_weight.shape[1])
     first = (taps[0] + taps[1] + taps[2]).T.astype(jnp.bfloat16)
     second = jnp.concatenate([taps[0] + taps[1], taps[2]], axis=0).T.astype(jnp.bfloat16)
-    place = jnp.asarray(placing_matrix(), jnp.bfloat16)
-    return decode(ids, tiles, place, first, second, norm_gain[:, None], norm_shift[:, None])
+    placing = jnp.asarray(placing_matrix(), jnp.bfloat16)
+    decoder = [first, second, norm_gain[:, None], norm_shift[:, None]]
+
+    half = tokens.shape[0] // 2
+    b_own = tokens[half:]
+    b_pair = jnp.concatenate([b_own, shift(b_own, xh=1)])
+    a_z = lax.all_gather(tokens[:half], "z", axis=0, tiled=True)
+    a_x = shift(a_z, xh=1)
+    b_all = lax.all_gather(b_pair, "z", axis=0, tiled=True)
+
+    q_scale = LOG2E * HEAD_DIM**-0.5
+
+    def both_cores(own, other):
+        return jnp.concatenate([own, shift(other, c=1)])
+
+    q1, kv1, q1_sent, kv1_sent = project([a_z], weights, q_scale)
+    q1, kv1 = both_cores(q1, q1_sent), both_cores(kv1, kv1_sent)
+    kv1_y = {n: shift(kv1, y=n) for n in (1, 3, 2)}
+    done_before = [q1, *kv1_y.values(), ids, w, noisy, *decoder]
+    q2, kv2, q2_sent, kv2_sent = project([a_x, b_all], weights, q_scale, done_before)
+    kv2 = both_cores(kv2, kv2_sent)
+    kv2_y = {n: shift(kv2, y=n) for n in (1, 3, 2)}
+
+    q1 = q1.reshape(1, 2, 4, half, HEAD_DIM)
+    q2 = both_cores(q2, q2_sent).reshape(2, 12 * half, HEAD_DIM)
+    q_a = jnp.concatenate([q1, q2[:, : 4 * half].reshape(1, 2, 4, half, HEAD_DIM)])
+    q_b = q2[:, 4 * half :].reshape(2, 4, 2, half, HEAD_DIM).transpose(2, 0, 1, 3, 4)
+    q_own = jnp.concatenate([q_a, q_b], axis=3).reshape(-1, HEAD_DIM)
+    q_other = shift(q_own, xl=1)
+
+    early = [kv1, kv2, kv1_y[1], kv1_y[3], kv1_y[2]]
+    q_both = jnp.concatenate([q_own, q_other])
+    carry = attention(q_own, early, rows_out=q_both.shape[0])
+    carry = attention(q_other, early, into=carry)
+    place = jnp.stack([coordinate["xl"], coordinate["xh"], coordinate["c"]])
+    parts = attention(q_both, [kv2_y[1], kv2_y[3], kv2_y[2]], carry, last=(place, w))
+    parts = parts.reshape(-1, PAYLOAD, 128)
+    parts = lax.all_to_all(parts, SEQ + ("xl",), split_axis=0, concat_axis=0, tiled=True)
+    tile = combine(parts, noisy, 64)
+
+    own_tiles = lax.all_to_all(tile, ("xh", "z", "y", "xl"), split_axis=0, concat_axis=0, tiled=True)
+    other_tiles = shift(own_tiles, c=1)
+    return decode(ids, own_tiles, other_tiles, placing, *decoder)
 
 
 def solution(mesh):

time: 282 us -> 233 us (0.83)
  the two profiles are of different devices: /device:TPU:9 before, /device:TPU:0 now
where the time goes in v2:
time: 233 us; the launch traced here: 231 us
  Pallas kernels  81.2 us (35%)
  blocking collectives  42.8 us (18%)
  waiting for transfers between devices  34.7 us (15%)
  local copies, waits for them, and re-layouts  22.6 us (10%)
  starting transfers between devices  18.7 us (8%)
  other arithmetic  15.9 us (7%)
  between operations  15 us (6%)
    pallas_call x3, Pallas kernels, attention(): pl.pallas_call(functools.partial(attention_kernel, bk, len(kvs), carry is...  51.1 us
    ppermute x15, waiting for transfers between devices, shift(): return lax.ppermute(x, AXES, pairs)  26.3 us
    all_to_all x1, blocking collectives, body(): lax.all_to_all(tile, ('xh', 'z', 'y', 'xl'), split_axis=0, concat_axis=0,...  23.6 us
    all_to_all x1, blocking collectives, body(): lax.all_to_all(parts, SEQ + ('xl',), split_axis=0, concat_axis=0, tiled=T...  19.2 us
    ppermute x15, starting transfers between devices, shift(): return lax.ppermute(x, AXES, pairs)  18.6 us
    pallas_call x1, Pallas kernels, decode(): pl.pallas_call(decode_kernel, grid_spec=pltpu.PrefetchScalarGridSpec(num_...  14.5 us
    pallas_call x2, Pallas kernels, project(): pl.pallas_call(functools.partial(project_kernel, steps, scale, len(after)...  13.3 us
    unnamed x48, local copies, waits for them, and re-layouts  8.75 us
  transfers between devices with their start and end apart: 17, of which 10 were waited for; matrix products, arithmetic and copies ran while one was open for 15% of the time, Pallas kernels for 12%

profile of v2, /device:TPU:0, one launch (start us, length us, event | category | flops | bytes accessed | tf_op | source)
XLA Modules:
  0.0 231.0 jit_solution(11240536975838883296)
XLA Ops:
  6.5 1.9 fusion.6
  8.6 3.2 %collective-permute-start.3 = (bf16[64,3072]{1,0:T(8,128)(2,1)S(1)}, bf16[64,3072]{1,0:T(8,128)(2,1)S(1)}, u32[]{:S(2)}, u32[]{:S(2)}) collective-permute-start(bf16[64,3072]{1,0:T(8,128)(2,1)S(1)} %get-tuple-element.31), channel_id=1, source_target_pairs={{0,64},{1,65},{2,66},{3,67},{4,68},{5,69},{6,70},{7,71},{8,72},{9,... | collective-permute-start | bytes 1179656 | tf_op jit(solution)/shard_map/ppermute | solution.py:37
  11.7 9.1 %collective-permute-done.3 = bf16[64,3072]{1,0:T(8,128)(2,1)S(1)} collective-permute-done((bf16[64,3072]{1,0:T(8,128)(2,1)S(1)}, bf16[64,3072]{1,0:T(8,128)(2,1)S(1)}, u32[]{:S(2)}, u32[]{:S(2)}) %collective-permute-start.3) | collective-permute-done | bytes 393248 | tf_op jit(solution)/shard_map/ppermute | solution.py:37
  21.8 2.9 %copy.21 = bf16[3,3072,128]{1,2,0:T(8,128)(2,1)S(1)} copy(bf16[3,3072,128]{2,1,0:T(8,128)(2,1)} %param.11) | data formatting | bytes 4718592 | tf_op args[1]
  24.8 1.2 copy.25
  30.3 2.6 %fusion.1 = (bf16[144,512]{0,1:T(8,128)(2,1)S(1)}, bf16[512,144]{1,0:T(8,128)(2,1)}) fusion(f32[432,512]{0,1:T(8,128)} %convert_element_type.12), kind=kLoop, calls=%fused_computation.11 | loop fusion | flops 294912 | bytes 1179648 | tf_op jit(solution)/shard_map/convert
  32.9 5.3 %all-gather.3.cloned.1.call-done.refs_0_ = bf16[256,3072]{1,0:T(8,128)(2,1)} async-done(((bf16[64,3072]{1,0:T(8,128)(2,1)}), bf16[256,3072]{1,0:T(8,128)(2,1)}) %all-gather.3.cloned.1.call-update) | async-done | bytes 1572880 | tf_op jit(solution)/shard_map/all_gather | solution.py:396
  38.3 3.0 %collective-permute-start.2 = (bf16[256,3072]{1,0:T(8,128)(2,1)}, bf16[256,3072]{1,0:T(8,128)(2,1)}, u32[]{:S(2)}, u32[]{:S(2)}) collective-permute-start(bf16[256,3072]{1,0:T(8,128)(2,1)} %all-gather.3.cloned.1.call-done.refs_0_), channel_id=1, source_target_pairs={{0,64},{1,65},{2,66},{3,67},{4,68},{5,69},{6,70},{7,71},{8,72},{9,... | collective-permute-start | bytes 4718600 | tf_op jit(solution)/shard_map/ppermute | solution.py:37
  42.8 4.3 %pad_maximum_fusion = bf16[6,3072,128]{1,2,0:T(8,128)(2,1)} fusion(bf16[3,3072,128]{1,2,0:T(8,128)(2,1)} %collective-permute-done, bf16[3,3072,128]{1,2,0:T(8,128)(2,1)S(1)} %copy.21), kind=kLoop, calls=%fused_computation.1 | loop fusion | flops 2359296 | bytes 9437184 | tf_op jit(solution)/shard_map/concatenate | solution.py:371
  47.1 6.7 %copy.22.refs_1_.refs_2_ = bf16[3072,768]{1,0:T(8,128)(2,1)} copy(bf16[3072,768]{0,1:T(8,128)(2,1)} %bitcast.35) | data formatting | bytes 9437184 | tf_op jit(solution)/shard_map/reshape | solution.py:372
  53.8 4.9 %project.2 = (bf16[256,128]{1,0:T(8,128)(2,1)}, bf16[256,256]{1,0:T(8,128)(2,1)}, bf16[256,128]{1,0:T(8,128)(2,1)}, bf16[256,256]{1,0:T(8,128)(2,1)}) custom-call(bf16[256,3072]{1,0:T(8,128)(2,1)} %all-gather.3.cloned.1.call-done.refs_0_, bf16[3072,768]{1,0:T(8,128)(2,1)} %copy.22.refs_1_.refs_2_), custom_call_target="tpu_custom_call" | custom-call | tf_op jit(solution)/shard_map/project/pallas_call | solution.py:71
  60.3 1.6 collective-permute-start.5
  61.9 1.7 collective-permute-start.6
  63.6 1.8 collective-permute-start.7
  71.2 5.4 %collective-permute-done.7.refs_6_.refs_5_ = bf16[512,256]{1,0:T(8,128)(2,1)S(1)} collective-permute-done((bf16[512,256]{1,0:T(8,128)(2,1)S(1)}, bf16[512,256]{1,0:T(8,128)(2,1)S(1)}, u32[]{:S(2)}, u32[]{:S(2)}) %collective-permute-start.7) | collective-permute-done | bytes 262176 | tf_op jit(solution)/shard_map/ppermute | solution.py:37
  76.6 3.1 %all-gather.5.cloned.1.call-done.refs_1_ = bf16[512,3072]{1,0:T(8,128)(2,1)} async-done(((bf16[128,3072]{1,0:T(8,128)(2,1)}), bf16[512,3072]{1,0:T(8,128)(2,1)}) %all-gather.5.cloned.1.call-update) | async-done | bytes 3145744 | tf_op jit(solution)/shard_map/all_gather | solution.py:398
  79.7 8.4 %project.3 = (bf16[768,128]{1,0:T(8,128)(2,1)}, bf16[768,256]{1,0:T(8,128)(2,1)}, bf16[768,128]{1,0:T(8,128)(2,1)}, bf16[768,256]{1,0:T(8,128)(2,1)}) custom-call(bf16[256,3072]{1,0:T(8,128)(2,1)} %collective-permute-done.2.refs_0_, bf16[512,3072]{1,0:T(8,128)(2,1)} %all-gather.5.cloned.1.call-done.refs_1_, bf16[3072,768]{1,0:T(8,128)(2,1)} %copy.22.refs_1_.refs_2_, ...), custom_call_target="tpu_custom_call" | custom-call | tf_op jit(solution)/shard_map/project/pallas_call | solution.py:71
  91.9 1.6 collective-permute-start.9
  93.5 1.6 collective-permute-start.11
  95.1 1.8 collective-permute-start.12
  96.8 1.8 collective-permute-start.13
  99.3 11.5 %attention.3 = (f32[4096,256]{1,0:T(8,128)}, f32[4096,128]{1,0:T(8,128)}) custom-call(bf16[2048,128]{1,0:T(8,128)(2,1)} %bitcast.37, bf16[512,256]{1,0:T(8,128)(2,1)} %copy-done.9, bf16[1536,256]{1,0:T(8,128)(2,1)} %copy-done.1, bf16[512,256]{1,0:T(8,128)(2,1)} %copy-done.5, bf16[512,256]{1,0:T(8,128)(2,1)} %copy-done.6, bf16[512,256]{1,0:T(8,128)(2,1)} %copy-done.7), custom_call_target="tpu_custom_call" | custom-call | tf_op jit(solution)/shard_map/attention/pallas_call | solution.py:200
  111.6 11.5 %attention.4 = (f32[4096,256]{1,0:T(8,128)}, f32[4096,128]{1,0:T(8,128)}) custom-call(bf16[2048,128]{1,0:T(8,128)(2,1)} %copy-done.8, bf16[512,256]{1,0:T(8,128)(2,1)} %copy-done.9, bf16[1536,256]{1,0:T(8,128)(2,1)} %copy-done.1, bf16[512,256]{1,0:T(8,128)(2,1)} %copy-done.5, ...), custom_call_target="tpu_custom_call", output_to_operand_aliasing={{0}: (6, {}), {1}: (7, {})} | custom-call | tf_op jit(solution)/shard_map/attention/pallas_call | solution.py:200
  123.1 2.1 pad_maximum_fusion.1.refs_1_
  125.2 5.0 %collective-permute-done.12.refs_3_ = bf16[1536,256]{1,0:T(8,128)(2,1)S(1)} collective-permute-done((bf16[1536,256]{1,0:T(8,128)(2,1)S(1)}, bf16[1536,256]{1,0:T(8,128)(2,1)S(1)}, u32[]{:S(2)}, u32[]{:S(2)}) %collective-permute-start.12) | collective-permute-done | bytes 786464 | tf_op jit(solution)/shard_map/ppermute | solution.py:37
  130.2 1.7 collective-permute-done.13.refs_4_
  132.8 28.0 %attention.5 = bf16[2,4,2,2,80,128]{5,4,3,2,1,0:T(8,128)(2,1)} custom-call(s32[3]{0:T(128)} %pad_add_fusion.1.refs_0_, bf16[4096,128]{1,0:T(8,128)(2,1)} %pad_maximum_fusion.1.refs_1_, bf16[1536,256]{1,0:T(8,128)(2,1)} %copy-done.12, bf16[1536,256]{1,0:T(8,128)(2,1)} %copy-done.13, bf16[1536,256]{1,0:T(8,128)(2,1)} %copy-done.14, ...), custom_call_target="tpu_custom_call" | custom-call | tf_op jit(solution)/shard_map/attention/pallas_call | solution.py:200
  160.9 19.2 %all_to_all.10.parts_ref = bf16[32,80,128]{2,1,0:T(8,128)(2,1)} all-to-all(bf16[32,80,128]{2,1,0:T(8,128)(2,1)} %bitcast.39), channel_id=1, replica_groups=mesh['xh'=2,'z'=4,'c'=2,'y'=4,'xl'=2] {'xh','z','c','xl'}, dimensions={0} | all-to-all | bytes 1310720 | tf_op jit(solution)/shard_map/all_to_all | solution.py:427
  180.1 2.3 %latent_tile.1 = bf16[64,64,128]{2,1,0:T(8,128)(2,1)} custom-call(bf16[32,80,128]{2,1,0:T(8,128)(2,1)} %all_to_all.10.parts_ref, f32[64,128]{1,0:T(8,128)} %bitcast.46), custom_call_target="tpu_custom_call" | custom-call | tf_op jit(solution)/shard_map/latent_tile/pallas_call | solution.py:237
  182.4 23.6 %all_to_all.11.own_ref = bf16[64,64,128]{2,1,0:T(8,128)(2,1)S(1)} all-to-all(bf16[64,64,128]{2,1,0:T(8,128)(2,1)} %latent_tile.1), channel_id=1, replica_groups=mesh['xh'=2,'z'=4,'c'=2,'y'=4,'xl'=2] {'xh','z','y','xl'}, dimensions={0} | all-to-all | bytes 2097152 | tf_op jit(solution)/shard_map/all_to_all | solution.py:430
  206.0 2.7 %collective-permute-done.14.other_ref = bf16[64,64,128]{2,1,0:T(8,128)(2,1)S(1)} collective-permute-done((bf16[64,64,128]{2,1,0:T(8,128)(2,1)S(1)}, bf16[64,64,128]{2,1,0:T(8,128)(2,1)S(1)}, u32[]{:S(2)}, u32[]{:S(2)}) %collective-permute-start.14) | collective-permute-done | bytes 1048608 | tf_op jit(solution)/shard_map/ppermute | solution.py:37
  209.7 14.5 %decode.1 = bf16[1,4,512,2048]{3,2,1,0:T(8,128)(2,1)} custom-call(s32[17]{0:T(128)} %pad_add_fusion.refs_7_.ids_ref, bf16[64,64,128]{2,1,0:T(8,128)(2,1)} %copy-done.4, bf16[64,64,128]{2,1,0:T(8,128)(2,1)} %copy-done.10, bf16[1024,1024]{1,0:T(8,128)(2,1)} %constant.90.clone.place_ref, bf16[512,144]{1,0:T(8,128)(2,1)} %get-tuple-element.30.refs_10_.first_ref, ...), custom_call_target="tpu_custom_call" | custom-call | tf_op jit(solution)/shard_map/decode/pallas_call | solution.py:329
  (94 shorter events, 20.0 us)
Async XLA Ops:
  6.5 52.2 %copy-start = (bf16[2048,64]{0,1:T(8,128)(2,1)S(1)}, bf16[2048,64]{0,1:T(8,128)(2,1)}, u32[]{:S(2)}) copy-start(bf16[2048,64]{0,1:T(8,128)(2,1)} %param.13) | copy-start | bytes 786436
  6.5 31.7 %all-gather.3.cloned.1.call-start = ((), (), s32[]{:S(2)}) async-start(), calls=%async_computation.2 | async-start | bytes 1966080 | tf_op jit(solution)/shard_map/all_gather | solution.py:396
  8.5 71.2 %all-gather.5.cloned.1.call-start = ((), (), s32[]{:S(2)}) async-start(), calls=%async_computation.3 | async-start | bytes 3932160 | tf_op jit(solution)/shard_map/all_gather | solution.py:398
  8.6 12.3 %collective-permute-start.3 = (bf16[64,3072]{1,0:T(8,128)(2,1)S(1)}, bf16[64,3072]{1,0:T(8,128)(2,1)S(1)}, u32[]{:S(2)}, u32[]{:S(2)}) collective-permute-start(bf16[64,3072]{1,0:T(8,128)(2,1)S(1)} %get-tuple-element.31), channel_id=1, source_target_pairs={{0,64},{1,65},{2,66},{3,67},{4,68},{5,69},{6,70},{7,71},{8,72},{9,... | collective-permute-start | bytes 1179656 | tf_op jit(solution)/shard_map/ppermute | solution.py:37
  24.7 4.1 %copy-start.17 = (s32[256,4]{0,1:T(4,128)S(1)}, s32[256,4]{0,1:T(4,128)}, u32[]{:S(2)}) copy-start(s32[256,4]{0,1:T(4,128)} %param.18) | copy-start | bytes 12292
  24.7 18.1 %collective-permute-start = (bf16[3,3072,128]{1,2,0:T(8,128)(2,1)S(1)}, bf16[3,3072,128]{1,2,0:T(8,128)(2,1)}, u32[]{:S(2)}, u32[]{:S(2)}) collective-permute-start(bf16[3,3072,128]{1,2,0:T(8,128)(2,1)S(1)} %copy.21), channel_id=1, source_target_pairs={{0,8},{1,9},{2,10},{3,11},{4,12},{5,13},{6,14},{7,15},{8,0},{9,1},... | collective-permute-start | bytes 7077896 | tf_op jit(solution)/shard_map/ppermute | solution.py:37
  38.3 38.3 %collective-permute-start.2 = (bf16[256,3072]{1,0:T(8,128)(2,1)}, bf16[256,3072]{1,0:T(8,128)(2,1)}, u32[]{:S(2)}, u32[]{:S(2)}) collective-permute-start(bf16[256,3072]{1,0:T(8,128)(2,1)} %all-gather.3.cloned.1.call-done.refs_0_), channel_id=1, source_target_pairs={{0,64},{1,65},{2,66},{3,67},{4,68},{5,69},{6,70},{7,71},{8,72},{9,... | collective-permute-start | bytes 4718600 | tf_op jit(solution)/shard_map/ppermute | solution.py:37
  53.8 13.5 %copy-start.18 = (f32[512]{0:T(512)S(1)}, f32[512]{0:T(512)}, u32[]{:S(2)}) copy-start(f32[512]{0:T(512)} %param.15) | copy-start | bytes 6148
  53.8 14.3 %copy-start.19 = (f32[512]{0:T(512)S(1)}, f32[512]{0:T(512)}, u32[]{:S(2)}) copy-start(f32[512]{0:T(512)} %param.16) | copy-start | bytes 6148
  53.8 15.2 %copy-start.16 = (f32[128,64]{0,1:T(8,128)S(1)}, f32[128,64]{0,1:T(8,128)}, u32[]{:S(2)}) copy-start(f32[128,64]{0,1:T(8,128)} %param.12) | copy-start | bytes 98308
  58.7 1.6 collective-permute-start.4
  60.3 27.8 %copy-start.9 = (bf16[512,256]{1,0:T(8,128)(2,1)}, bf16[512,256]{1,0:T(8,128)(2,1)S(1)}, u32[]{:S(2)}) copy-start(bf16[512,256]{1,0:T(8,128)(2,1)S(1)} %constant_dynamic-update-slice_fusion.2.refs_1_) | copy-start | bytes 786436
  60.3 10.8 %collective-permute-start.5 = (bf16[512,256]{1,0:T(8,128)(2,1)S(1)}, bf16[512,256]{1,0:T(8,128)(2,1)S(1)}, u32[]{:S(2)}, u32[]{:S(2)}) collective-permute-start(bf16[512,256]{1,0:T(8,128)(2,1)S(1)} %constant_dynamic-update-slice_fusion.2.refs_1_), channel_id=1, source_target_pairs={{0,2},{1,3},{2,4},{3,5},{4,6},{5,7},{6,0},{7,1},{8,10},{9,11},{10,... | collective-permute-start | bytes 786440 | tf_op jit(solution)/shard_map/ppermute | solution.py:37
  61.9 9.2 %collective-permute-start.6 = (bf16[512,256]{1,0:T(8,128)(2,1)S(1)}, bf16[512,256]{1,0:T(8,128)(2,1)S(1)}, u32[]{:S(2)}, u32[]{:S(2)}) collective-permute-start(bf16[512,256]{1,0:T(8,128)(2,1)S(1)} %constant_dynamic-update-slice_fusion.2.refs_1_), channel_id=1, source_target_pairs={{0,6},{1,7},{2,0},{3,1},{4,2},{5,3},{6,4},{7,5},{8,14},{9,15},{10,... | collective-permute-start | bytes 786440 | tf_op jit(solution)/shard_map/ppermute | solution.py:37
  63.6 12.9 %collective-permute-start.7 = (bf16[512,256]{1,0:T(8,128)(2,1)S(1)}, bf16[512,256]{1,0:T(8,128)(2,1)S(1)}, u32[]{:S(2)}, u32[]{:S(2)}) collective-permute-start(bf16[512,256]{1,0:T(8,128)(2,1)S(1)} %constant_dynamic-update-slice_fusion.2.refs_1_), channel_id=1, source_target_pairs={{0,4},{1,5},{2,6},{3,7},{4,0},{5,1},{6,2},{7,3},{8,12},{9,13},{10,... | collective-permute-start | bytes 786440 | tf_op jit(solution)/shard_map/ppermute | solution.py:37
  69.6 1.5 collective-permute-start.1
  71.1 8.6 %copy-start.11 = (bf16[512,128]{1,0:T(8,128)(2,1)}, bf16[512,128]{1,0:T(8,128)(2,1)S(1)}, u32[]{:S(2)}) copy-start(bf16[512,128]{1,0:T(8,128)(2,1)S(1)} %constant_dynamic-update-slice_fusion.refs_3_) | copy-start | bytes 393220
  71.1 8.6 %copy-start.5 = (bf16[512,256]{1,0:T(8,128)(2,1)}, bf16[512,256]{1,0:T(8,128)(2,1)S(1)}, u32[]{:S(2)}) copy-start(bf16[512,256]{1,0:T(8,128)(2,1)S(1)} %collective-permute-done.5.refs_4_.refs_3_) | copy-start | bytes 786436
  71.1 8.5 %copy-start.6 = (bf16[512,256]{1,0:T(8,128)(2,1)}, bf16[512,256]{1,0:T(8,128)(2,1)S(1)}, u32[]{:S(2)}) copy-start(bf16[512,256]{1,0:T(8,128)(2,1)S(1)} %collective-permute-done.6.refs_5_.refs_4_) | copy-start | bytes 786436
  76.6 3.1 %copy-start.7 = (bf16[512,256]{1,0:T(8,128)(2,1)}, bf16[512,256]{1,0:T(8,128)(2,1)S(1)}, u32[]{:S(2)}) copy-start(bf16[512,256]{1,0:T(8,128)(2,1)S(1)} %collective-permute-done.7.refs_6_.refs_5_) | copy-start | bytes 786436
  88.1 5.3 %copy-start.15 = (bf16[768,256]{1,0:T(8,128)(2,1)S(1)}, bf16[768,256]{1,0:T(8,128)(2,1)}, u32[]{:S(2)}) copy-start(bf16[768,256]{1,0:T(8,128)(2,1)} %get-tuple-element.23) | copy-start | bytes 1179652
  88.1 1.7 collective-permute-start.8
  88.2 5.2 %collective-permute-start.10 = (bf16[768,256]{1,0:T(8,128)(2,1)}, bf16[768,256]{1,0:T(8,128)(2,1)S(1)}, u32[]{:S(2)}, u32[]{:S(2)}) collective-permute-start(bf16[768,256]{1,0:T(8,128)(2,1)} %get-tuple-element.24), channel_id=1, source_target_pairs={{0,8},{1,9},{2,10},{3,11},{4,12},{5,13},{6,14},{7,15},{8,0},{9,1},... | collective-permute-start | bytes 1179656 | tf_op jit(solution)/shard_map/ppermute | solution.py:37
  91.8 7.4 %copy-start.2 = (bf16[2,2,4,128,128]{4,3,2,1,0:T(8,128)(2,1)}, bf16[2,2,4,128,128]{4,3,2,1,0:T(8,128)(2,1)S(1)}, u32[]{:S(2)}) copy-start(bf16[2,2,4,128,128]{4,3,2,1,0:T(8,128)(2,1)S(1)} %copy.30) | copy-start | bytes 1572868
  91.9 18.9 %collective-permute-start.9 = (bf16[2048,128]{1,0:T(8,128)(2,1)S(1)}, bf16[2048,128]{1,0:T(8,128)(2,1)S(1)}, u32[]{:S(2)}, u32[]{:S(2)}) collective-permute-start(bf16[2048,128]{1,0:T(8,128)(2,1)S(1)} %bitcast.36), channel_id=1, source_target_pairs={{0,1},{1,0},{2,3},{3,2},{4,5},{5,4},{6,7},{7,6},{8,9},{9,8},{10,11... | collective-permute-start | bytes 1572872 | tf_op jit(solution)/shard_map/ppermute | solution.py:37
  93.5 5.8 %copy-start.1 = (bf16[1536,256]{1,0:T(8,128)(2,1)}, bf16[1536,256]{1,0:T(8,128)(2,1)S(1)}, u32[]{:S(2)}) copy-start(bf16[1536,256]{1,0:T(8,128)(2,1)S(1)} %constant_dynamic-update-slice_fusion.4.refs_2_) | copy-start | bytes 2359300
  93.5 31.7 %collective-permute-start.11 = (bf16[1536,256]{1,0:T(8,128)(2,1)S(1)}, bf16[1536,256]{1,0:T(8,128)(2,1)S(1)}, u32[]{:S(2)}, u32[]{:S(2)}) collective-permute-start(bf16[1536,256]{1,0:T(8,128)(2,1)S(1)} %constant_dynamic-update-slice_fusion.4.refs_2_), channel_id=1, source_target_pairs={{0,2},{1,3},{2,4},{3,5},{4,6},{5,7},{6,0},{7,1},{8,10},{9,11},{10,... | collective-permute-start | bytes 2359304 | tf_op jit(solution)/shard_map/ppermute | solution.py:37
  95.1 35.2 %collective-permute-start.12 = (bf16[1536,256]{1,0:T(8,128)(2,1)S(1)}, bf16[1536,256]{1,0:T(8,128)(2,1)S(1)}, u32[]{:S(2)}, u32[]{:S(2)}) collective-permute-start(bf16[1536,256]{1,0:T(8,128)(2,1)S(1)} %constant_dynamic-update-slice_fusion.4.refs_2_), channel_id=1, source_target_pairs={{0,6},{1,7},{2,0},{3,1},{4,2},{5,3},{6,4},{7,5},{8,14},{9,15},{10,... | collective-permute-start | bytes 2359304 | tf_op jit(solution)/shard_map/ppermute | solution.py:37
  96.8 35.1 %collective-permute-start.13 = (bf16[1536,256]{1,0:T(8,128)(2,1)S(1)}, bf16[1536,256]{1,0:T(8,128)(2,1)S(1)}, u32[]{:S(2)}, u32[]{:S(2)}) collective-permute-start(bf16[1536,256]{1,0:T(8,128)(2,1)S(1)} %constant_dynamic-update-slice_fusion.4.refs_2_), channel_id=1, source_target_pairs={{0,4},{1,5},{2,6},{3,7},{4,0},{5,1},{6,2},{7,3},{8,12},{9,13},{10,... | collective-permute-start | bytes 2359304 | tf_op jit(solution)/shard_map/ppermute | solution.py:37
  111.6 11.5 %copy-start.3 = (bf16[2,2,4,128,128]{4,3,2,1,0:T(8,128)(2,1)S(1)}, bf16[2,2,4,128,128]{4,3,2,1,0:T(8,128)(2,1)}, u32[]{:S(2)}) copy-start(bf16[2,2,4,128,128]{4,3,2,1,0:T(8,128)(2,1)} %copy-done.2) | copy-start | bytes 1572868
  125.2 6.7 %copy-start.12 = (bf16[1536,256]{1,0:T(8,128)(2,1)}, bf16[1536,256]{1,0:T(8,128)(2,1)S(1)}, u32[]{:S(2)}) copy-start(bf16[1536,256]{1,0:T(8,128)(2,1)S(1)} %collective-permute-done.11.refs_2_) | copy-start | bytes 2359300
  206.0 2.7 %collective-permute-start.14 = (bf16[64,64,128]{2,1,0:T(8,128)(2,1)S(1)}, bf16[64,64,128]{2,1,0:T(8,128)(2,1)S(1)}, u32[]{:S(2)}, u32[]{:S(2)}) collective-permute-start(bf16[64,64,128]{2,1,0:T(8,128)(2,1)S(1)} %all_to_all.11.own_ref), channel_id=1, source_target_pairs={{0,8},{1,9},{2,10},{3,11},{4,12},{5,13},{6,14},{7,15},{8,0},{9,1},... | collective-permute-start | bytes 3145736 | tf_op jit(solution)/shard_map/ppermute | solution.py:37
  (6 other events, 9.7 us)
Sparse Core Ops, SparseCore 0:
  9.0 29.1 all-gather.2
  39.9 39.7 all-gather.4
